TPU v7x, 128 devices: a whole 4x4x4 slice. The times are simulated.
128 devices in a mesh: ctx: 32 (over y, x, core), head: 4 (over z).
Axes of the slice: x: 4, y: 4, z: 4, core: 2. Of those that a mesh axis runs over, the one named last changes fastest.
Arguments:
- queries: bfloat16 [16384, 4096], P('ctx', 'head'), may hold values from -6 to 6
- keys: bfloat16 [16384, 1024], P('ctx', 'head'), may hold values from -6 to 6
- values: bfloat16 [16384, 1024], P('ctx', 'head'), may hold values from -6 to 6
- lengths: int32 [8], replicated, may hold values from 1 to 8192, 16384 in all
- out_weight: bfloat16 [4096, 8192], P('head'), may hold values from -0.125 to 0.125
Outputs:
- mixed: bfloat16 [16384, 8192], P('ctx', 'head')
Inputs may be any that keep to these rules, and one draw needn't show every extreme that they name: Positive document lengths that sum to 16384; the longest is exactly 8192.
All inputs are finite; a program needn't handle non-finite values.
Results may differ from a plain program's by a relative error of at most 0.0065.
The roundings to bfloat16 on the way count: a program that leaves them out, or rounds other values in their place, can miss the bound.
Values may be sent and summed in bfloat16 or wider, within the bound.
A program may use at most 128 MiB of HBM per device.

v0:
```python
import math

import jax
import jax.numpy as jnp
from jax import lax
from jax.sharding import PartitionSpec as P

rope_base = 1000000.0
ramp_low = 23.0
ramp_high = 40.0
yarn_factor = 4.0
mscale = 0.1 * math.log(4.0) + 1.0
neg_large = -1e30


def doc_starts(positions, lengths):
    doc_ends = jnp.cumsum(lengths)
    picked = jnp.where(positions[:, None] >= doc_ends[None, :], lengths[None, :], 0)
    return jnp.sum(picked, axis=1)


def apply_rotary(heads, start_offsets):
    pair_index = jnp.arange(64).astype(jnp.float32)
    extrap = jnp.exp(-(2.0 * pair_index / 128.0) * math.log(rope_base))
    ramp = jnp.clip((pair_index - ramp_low) / (ramp_high - ramp_low), 0.0, 1.0)
    inverse = extrap / yarn_factor * ramp + extrap * (1.0 - ramp)
    angles = start_offsets.astype(jnp.float32)[:, None] * inverse[None, :]
    cosine = (jnp.cos(angles) * mscale)[:, None, :]
    sine = (jnp.sin(angles) * mscale)[:, None, :]
    first_half = heads[..., :64]
    second_half = heads[..., 64:]
    return jnp.concatenate(
        [first_half * cosine - second_half * sine, second_half * cosine + first_half * sine],
        axis=-1,
    )


def per_device(queries, keys, values, lengths, out_weight):
    tok_rows = queries.shape[0]
    kv_width = keys.shape[1]
    kv_heads = kv_width // 128
    q_heads = queries.shape[1] // 128
    query_group = q_heads // kv_heads
    scale = 1.0 / math.sqrt(128.0)
    device = lax.axis_index("ctx")
    first = device * tok_rows
    positions = first + jnp.arange(tok_rows)
    qstart = doc_starts(positions, lengths)
    start_offsets = positions - qstart
    query_rotated = apply_rotary(
        queries.astype(jnp.float32).reshape(tok_rows, q_heads, 128), start_offsets
    ).astype(jnp.bfloat16)
    query_rotated = query_rotated.reshape(tok_rows, kv_heads, query_group, 128)
    key_rotated = apply_rotary(
        keys.astype(jnp.float32).reshape(tok_rows, kv_heads, 128), start_offsets
    ).astype(jnp.bfloat16)
    key_rotated = key_rotated.reshape(tok_rows, kv_width)
    lowest = qstart[0]
    highest = first + tok_rows - 1

    def attend(carry, key_block, value_block, key_first):
        count_rows = key_block.shape[0]
        needed = (key_first <= highest) & (key_first + count_rows - 1 >= lowest)

        def compute(state):
            run_max, run_sum, run_acc = state
            kheads = key_block.reshape(count_rows, kv_heads, 128)
            vheads = value_block.reshape(count_rows, kv_heads, 128)
            scores = (
                jnp.einsum(
                    "qgha,kga->ghqk", query_rotated, kheads, preferred_element_type=jnp.float32
                )
                * scale
            )
            kpos = key_first + jnp.arange(count_rows)
            visible = (kpos[None, :] <= positions[:, None]) & (kpos[None, :] >= qstart[:, None])
            scores = jnp.where(visible, scores, neg_large)
            new_max = jnp.maximum(run_max, jnp.max(scores, axis=-1))
            weights = jnp.where(visible, jnp.exp(scores - new_max[..., None]), 0.0)
            rescale = jnp.exp(run_max - new_max)
            new_sum = run_sum * rescale + jnp.sum(weights, axis=-1)
            summed = jnp.einsum(
                "ghqk,kga->ghqa",
                weights.astype(jnp.bfloat16),
                vheads,
                preferred_element_type=jnp.float32,
            )
            return (new_max, new_sum, run_acc * rescale[..., None] + summed)

        def unchanged(state):
            return state

        return lax.cond(needed, compute, unchanged, carry)

    initial = (
        jnp.full((kv_heads, query_group, tok_rows), neg_large, jnp.float32),
        jnp.zeros((kv_heads, query_group, tok_rows), jnp.float32),
        jnp.zeros((kv_heads, query_group, tok_rows, 128), jnp.float32),
    )
    piece = (
        lax.all_gather(key_rotated, "ctx", axis=0, tiled=True),
        lax.all_gather(values, "ctx", axis=0, tiled=True),
    )
    total_rows = piece[0].shape[0]
    block_rows = min(total_rows, tok_rows)

    def inner(turn, state):
        offset = (turn * block_rows).astype(jnp.int32)
        key_block = lax.dynamic_slice_in_dim(piece[0], offset, block_rows, 0)
        value_block = lax.dynamic_slice_in_dim(piece[1], offset, block_rows, 0)
        return attend(state, key_block, value_block, offset)

    result = lax.fori_loop(0, total_rows // block_rows, inner, initial)
    run_max, run_sum, run_acc = result
    attended = run_acc / run_sum[..., None]
    attended = (
        jnp.transpose(attended, (2, 0, 1, 3)).astype(jnp.bfloat16).reshape(tok_rows, q_heads * 128)
    )
    partial_sums = jnp.dot(attended, out_weight, preferred_element_type=jnp.float32)
    return lax.psum_scatter(partial_sums, "head", scatter_dimension=1, tiled=True).astype(
        jnp.bfloat16
    )


def solution(mesh):
    return jax.shard_map(
        per_device,
        mesh=mesh,
        in_specs=(P("ctx", "head"), P("ctx", "head"), P("ctx", "head"), P(), P("head", None)),
        out_specs=P("ctx", "head"),
        check_vma=False,
    )
```

profile of v0, /device:TPU:16, one launch (start us, length us, event | category | flops | bytes accessed | tf_op | source)
XLA Modules:
  0.0 476.3 jit_solution(10917265864156446986)
XLA Ops:
  6.5 0.0 all-gather.5.cloned.1.call-start
  6.5 1.8 copy.40
  8.3 0.0 copy-start
  8.3 0.0 all-gather.5.cloned.1.call-update
  8.4 0.0 all-gather.3.cloned.1.call-start
  8.4 1.2 copy.49
  9.6 0.8 reduce-window.8
  10.4 0.7 select_reduce_fusion
  11.2 0.5 fusion.13
  11.7 0.1 subtract_convert_fusion.1
  11.8 0.7 pad_maximum_fusion.1
  12.6 0.0 all-gather.3.cloned.1.call-update
  12.6 0.0 reduce-scatter.2.cloned.1.call-start
  12.6 0.5 slice.15
  13.2 0.1 copy.37
  13.3 0.1 copy.39
  13.4 0.0 copy-done
  13.4 0.2 convert_bitcast_fusion
  13.7 0.5 copy.52
  14.2 0.7 fusion.15
  14.8 0.8 subtract_convert_fusion
  15.6 0.6 pad_maximum_fusion
  16.2 53.4 %all-gather.5.cloned.1.call-done = bf16[16384,256]{0,1:T(8,128)(2,1)} async-done(((bf16[512,256]{0,1:T(8,128)(2,1)}), bf16[16384,256]{0,1:T(8,128)(2,1)}) %all-gather.5.cloned.1.call-update) | async-done | bytes 8388624 | tf_op jit(solution)/shard_map/all_gather | solution.py:102
  69.6 61.4 %all-gather.3.cloned.1.call-done = bf16[16384,256]{0,1:T(8,128)(2,1)} async-done(((bf16[512,256]{0,1:T(8,128)(2,1)}), bf16[16384,256]{0,1:T(8,128)(2,1)}) %all-gather.3.cloned.1.call-update) | async-done | bytes 8388624 | tf_op jit(solution)/shard_map/all_gather | solution.py:101
  131.0 0.1 broadcast_in_dim.62
  131.1 29.8 %while.22 = (s32[]{:T(128)}, f32[2,4,512]{2,1,0:T(4,128)S(1)}, f32[2,4,512]{2,1,0:T(4,128)S(1)}, f32[2,4,512,128]{3,2,1,0:T(8,128)S(1)}, s32[]{:T(128)}, /*index...) while((s32[]{:T(128)}, f32[2,4,512]{2,1,0:T(4,128)S(1)}, ...), condition=%wide.region_7.8_spmd.clone, body=%wide.region_2.7_spmd.clone.sunk | while | flops 1102849024 | bytes 33306988 | solution.py:113
  142.2 9.2 %conditional.3 = ((f32[2,4,512]{2,1,0:T(4,128)S(1)}, f32[2,4,512]{2,1,0:T(4,128)S(1)}, f32[2,4,512,128]{3,2,1,0:T(8,128)S(1)})) conditional(s32[]{:T(128)} %convert_element_type.68, (f32[2,4,512]{2,1,0:T(4,128)S(1)}, f32[2,4,512]{2,1,0:T(4,128)S(1)}, f32[2,4,512,128]{3,2,1,0:T(8,128)S(1)}) %tuple.81, (s32[]{:T(128)}, s32[]{:T(128)}, ...), branch_computations={%region_3.3_spmd, %region_4.6_spmd} | conditional | flops 1102849024 | bytes 33304654 | solution.py:93
  142.2 0.3 compare_and_fusion
  142.5 1.1 constant_dynamic-slice_fusion
  143.6 2.1 fusion.2
  145.6 2.0 fusion.4
  147.7 3.6 multiply_add_fusion
  161.0 1.8 copy.41
  162.8 1.9 divide_convert_fusion
  164.7 15.8 %fusion.16 = f32[512,8192]{1,0:T(8,128)} fusion(bf16[512,1024]{0,1:T(8,128)(2,1)S(1)} %bitcast.49, bf16[1024,8192]{1,0:T(8,128)(2,1)} %param.13), kind=kOutput, calls=%fused_computation.36 | convolution fusion | flops 8589934592 | bytes 34603008 | tf_op jit(solution)/shard_map/dot_general | solution.py:119
  180.4 0.0 reduce-scatter.2.cloned.1.call-update
  180.5 285.4 %reduce-scatter.2.cloned.1.call-done = f32[512,2048]{1,0:T(8,128)} async-done(((f32[512,8192]{1,0:T(8,128)}), f32[512,2048]{1,0:T(8,128)}) %reduce-scatter.2.cloned.1.call-update) | async-done | bytes 4194320 | tf_op jit(solution)/shard_map/reduce_scatter | solution.py:120
  465.9 3.8 convert_element_type.58
  (72 shorter events, 0.7 us)
Async XLA Ops:
  6.5 63.1 %all-gather.5.cloned.1.call-start = ((), (), s32[]{:S(2)}) async-start(), calls=%async_computation.2 | async-start | bytes 8650752 | tf_op jit(solution)/shard_map/all_gather | solution.py:102
  8.3 5.1 %copy-start = (bf16[512,1024]{1,0:T(8,128)(2,1)S(1)}, bf16[512,1024]{1,0:T(8,128)(2,1)}, u32[]{:S(2)}) copy-start(bf16[512,1024]{1,0:T(8,128)(2,1)} %param.9) | copy-start | bytes 3145732
  8.4 122.6 %all-gather.3.cloned.1.call-start = ((), (), s32[]{:S(2)}) async-start(), calls=%async_computation.1 | async-start | bytes 8650752 | tf_op jit(solution)/shard_map/all_gather | solution.py:101
  12.6 453.3 %reduce-scatter.2.cloned.1.call-start = ((), (), s32[]{:S(2)}) async-start(), calls=%async_computation.3 | async-start | bytes 20971520 | tf_op jit(solution)/shard_map/reduce_scatter | solution.py:120
Sparse Core Ops, SparseCore 0:
  9.5 60.0 all-gather.4
  71.8 59.1 all-gather.2
  180.6 285.2 reduce-scatter.1
where the time goes:
time: 483 us; the launch traced here: 476 us
  waiting for transfers between devices  400 us (83%)
  matrix products  21.5 us (4%)
  loops' own time  20.6 us (4%)
  between operations  13.2 us (3%)
  other arithmetic  12.6 us (3%)
  local copies, waits for them, and re-layouts  7.98 us (2%)
    reduce_scatter x1, waiting for transfers between devices, per_device(): lax.psum_scatter(partial_sums, 'head', scatter_dimension=1, tiled=True)  285 us
    all_gather x1, waiting for transfers between devices, per_device(): lax.all_gather(key_rotated, 'ctx', axis=0, tiled=True)  61.4 us
    all_gather x1, waiting for transfers between devices, per_device(): lax.all_gather(values, 'ctx', axis=0, tiled=True)  53.4 us
    another operation x1, loops' own time, per_device(): result = lax.fori_loop(0, total_rows // block_rows, inner, initial)  20 us
    dot_general x1, matrix products, per_device(): jnp.dot(attended, out_weight, preferred_element_type=jnp.float32)  15.8 us
  transfers between devices with their start and end apart: 3, of which 3 were waited for; matrix products, arithmetic and copies ran while one was open for 2% of the time, Pallas kernels for 0%

commit v1 on v0

v1 whole, which is shorter than its diff:
```python
import functools
import math

import jax
import jax.numpy as jnp
from jax import lax
from jax.experimental import pallas as pl
from jax.experimental.pallas import tpu as pltpu
from jax.sharding import PartitionSpec as P

f32, bf16 = jnp.float32, jnp.bfloat16
rope_base = 1000000.0
ramp_low = 23.0
ramp_high = 40.0
yarn_factor = 4.0
mscale = 0.1 * math.log(4.0) + 1.0
neg_large = -1e30
exp2_scale = math.log2(math.e) / math.sqrt(128.0)
doc_penalty = 131072.0

NDOCS = 8
BLOCK = 1024
GROUP = 4
TILE = 1024


def doc_bounds(lengths):
    index = jnp.arange(NDOCS)
    ends = jnp.sum(jnp.where(index[None, :] <= index[:, None], lengths[None, :], 0), axis=1)
    return ends - lengths, ends


def doc_one_hot(positions, starts, ends):
    pad = 128 - NDOCS
    starts = jnp.pad(starts, (0, pad))[None, :]
    ends = jnp.pad(ends, (0, pad))[None, :]
    at = positions[:, None]
    return ((at >= starts) & (at < ends)).astype(f32)


def rotary_tables(start_offsets):
    pair_index = jnp.arange(64).astype(f32)
    extrap = jnp.exp(-(2.0 * pair_index / 128.0) * math.log(rope_base))
    ramp = jnp.clip((pair_index - ramp_low) / (ramp_high - ramp_low), 0.0, 1.0)
    inverse = extrap / yarn_factor * ramp + extrap * (1.0 - ramp)
    angles = start_offsets.astype(f32)[:, None] * inverse[None, :]
    return jnp.cos(angles) * mscale, jnp.sin(angles) * mscale


def rotate(heads, cosine, sine):
    cosine, sine = cosine[:, None, :], sine[:, None, :]
    first = heads[..., :64].astype(f32)
    second = heads[..., 64:].astype(f32)
    return jnp.concatenate(
        [first * cosine - second * sine, second * cosine + first * sine], axis=-1
    ).astype(bf16)


def attention_kernel(first_ref, q_ref, k_ref, v_ref, o_ref, top, total, acc):
    own = first_ref[1]

    def step(block, tile, diagonal):
        cols = pl.ds(pl.multiple_of(tile * TILE, TILE), TILE)
        keys = k_ref[pl.ds(pl.multiple_of(block * BLOCK, BLOCK), BLOCK), :]
        s = jnp.dot(keys, q_ref[:, cols], preferred_element_type=f32)
        if diagonal:
            at = lax.broadcasted_iota(jnp.int32, s.shape, 0)
            query = lax.broadcasted_iota(jnp.int32, s.shape, 1)
            s = jnp.where(at <= query, s, neg_large)
            new = jnp.max(s, axis=0, keepdims=True)
        else:
            old = top[:, cols]
            new = jnp.maximum(old, jnp.max(s, axis=0, keepdims=True))
        p = jnp.exp2((s - new) * exp2_scale)
        if diagonal:
            total[:, cols] = jnp.sum(p, axis=0, keepdims=True)
        else:
            scale = jnp.exp2((old - new) * exp2_scale)
            total[:, cols] = total[:, cols] * scale + jnp.sum(p, axis=0, keepdims=True)
        top[:, cols] = new
        values = v_ref[pl.ds(pl.multiple_of(block * 128, 128), 128), :]
        summed = jnp.dot(values, p.astype(bf16), preferred_element_type=f32)
        acc[:, cols] = summed if diagonal else acc[:, cols] * scale + summed

    def diagonal_tile(tile, _):
        step(own, tile, True)
        return 0

    lax.fori_loop(0, GROUP * BLOCK // TILE, diagonal_tile, 0)

    def one_block(block, _):
        def one_tile(tile, _):
            step(block, tile, False)
            return 0

        return lax.fori_loop(0, GROUP * BLOCK // TILE, one_tile, 0)

    lax.fori_loop(first_ref[0], own, one_block, 0)
    o_ref[...] = (acc[...] / total[...]).astype(bf16)


def attention(first, q, k, v):
    vmem = pl.BlockSpec(memory_space=pltpu.VMEM)
    columns = q.shape[1]
    return pl.pallas_call(
        attention_kernel,
        out_shape=jax.ShapeDtypeStruct((128, columns), bf16),
        in_specs=[pl.BlockSpec(memory_space=pltpu.SMEM), vmem, vmem, vmem],
        out_specs=vmem,
        scratch_shapes=[
            pltpu.VMEM((1, columns), f32),
            pltpu.VMEM((1, columns), f32),
            pltpu.VMEM((128, columns), f32),
        ],
        compiler_params=pltpu.CompilerParams(vmem_limit_bytes=52 * 2**20),
    )(first, q, k, v)


def per_device(queries, keys, values, lengths, out_weight):
    device = lax.axis_index("ctx")
    z = lax.axis_index("head")
    core = device % 2
    chip = device // 2
    other = 1 - core
    swap = [(i, i ^ 1) for i in range(32)]
    parity = [[i for i in range(32) if i % 2 == c] for c in (0, 1)]

    def part(x, width, which):
        return lax.dynamic_slice_in_dim(x, which * width, width, 1)

    rows = lax.dynamic_slice_in_dim(out_weight, core * 512, 512, 0)
    weights = [part(rows, 2048, z)]
    for shift in (1, 2, 3):
        block = part(rows, 2048, (z + shift) % 4)
        weights.append(lax.ppermute(block, "head", [(i, (i + shift) % 4) for i in range(4)]))

    mine = jnp.concatenate([part(queries, 512, core), part(keys, 128, core), part(values, 128, core)], 1)
    theirs = jnp.concatenate([part(queries, 512, other), part(keys, 128, other), part(values, 128, other)], 1)
    came = lax.ppermute(theirs, "ctx", swap)
    both = jnp.where(core == 0, jnp.concatenate([mine, came], 0), jnp.concatenate([came, mine], 0))

    starts, ends = doc_bounds(lengths)
    positions = chip * BLOCK + jnp.arange(BLOCK)
    one_hot = doc_one_hot(positions, starts, ends)
    qstart = jnp.sum(jnp.where(positions[:, None] >= ends[None, :], lengths[None, :], 0), axis=1)
    cosine, sine = rotary_tables(positions - qstart)
    turned = rotate(both[:, :640].reshape(BLOCK, 5, 128), cosine, sine)
    q = jnp.transpose(turned[:, :4], (2, 1, 0)).reshape(128, GROUP * BLOCK)
    penalty = jnp.transpose((one_hot - 1.0) * doc_penalty).astype(bf16)
    q = jnp.concatenate([q, jnp.tile(penalty, (1, GROUP))], 0)
    k = lax.all_gather(turned[:, 4], "ctx", axis=0, tiled=True, axis_index_groups=parity)
    v = lax.all_gather(both[:, 640:].T, "ctx", axis=0, tiled=True, axis_index_groups=parity)
    hot = doc_one_hot(jnp.arange(16 * BLOCK), starts, ends).astype(bf16)
    k = jnp.concatenate([k, hot], 1)
    first = jnp.stack([qstart[0] // BLOCK, chip]).astype(jnp.int32)
    attended = attention(first, q, k, v)

    attended = jnp.transpose(attended.reshape(128, GROUP, BLOCK), (2, 1, 0)).reshape(BLOCK, 512)
    gathered = lax.all_gather(attended, "head", axis=0)
    partial = 0.0
    for shift in range(4):
        source = (z - shift + 4) % 4
        from_z = lax.dynamic_index_in_dim(gathered, source, 0, keepdims=False)
        partial = partial + jnp.dot(from_z, weights[shift], preferred_element_type=f32)
    kept = lax.dynamic_slice_in_dim(partial, core * 512, 512, 0)
    sent = lax.dynamic_slice_in_dim(partial, other * 512, 512, 0)
    return (kept + lax.ppermute(sent, "ctx", swap)).astype(bf16)


def solution(mesh):
    return jax.shard_map(
        per_device,
        mesh=mesh,
        in_specs=(P("ctx", "head"), P("ctx", "head"), P("ctx", "head"), P(), P("head", None)),
        out_specs=P("ctx", "head"),
        check_vma=False,
    )
```

time: 483 us -> 377 us (0.78)
  the two profiles are of different devices: /device:TPU:16 before, /device:TPU:31 now
where the time goes in v1:
time: 377 us
  waiting for transfers between devices  201 us (53%)
  Pallas kernels  71.2 us (19%)
  other arithmetic  29.4 us (8%)
  matrix products  28.7 us (8%)
  local copies, waits for them, and re-layouts  23.6 us (6%)
  between operations  16 us (4%)
  starting transfers between devices  7.12 us (2%)
    all_gather x1, waiting for transfers between devices, per_device(): gathered = lax.all_gather(attended, 'head', axis=0)  111 us
    pallas_call x1, Pallas kernels, attention(): pl.pallas_call(attention_kernel, out_shape=jax.ShapeDtypeStruct((128, col...  71.2 us
    all_gather x1, waiting for transfers between devices, per_device(): lax.all_gather(both[:, 640:].T, 'ctx', axis=0, tiled=True, axis_index_gro...  46.1 us
    all_gather x1, waiting for transfers between devices, per_device(): lax.all_gather(turned[:, 4], 'ctx', axis=0, tiled=True, axis_index_groups...  36.5 us
    dot_general x4, matrix products, per_device(): jnp.dot(from_z, weights[shift], preferred_element_type=f32)  28.7 us
    dynamic_slice x3, local copies, waits for them, and re-layouts, part(): return lax.dynamic_slice_in_dim(x, which * width, width, 1)  11.4 us
  transfers between devices with their start and end apart: 8, of which 4 were waited for; matrix products, arithmetic and copies ran while one was open for 13% of the time, Pallas kernels for 0%

profile of v1, /device:TPU:31, one launch (start us, length us, event | category | flops | bytes accessed | tf_op | source)
XLA Modules:
  0.0 376.9 jit_solution(14262962797817052312)
XLA Ops:
  6.5 1.1 constant_dynamic-slice_fusion.4
  7.7 0.1 copy.52
  7.8 0.1 copy.51
  7.9 1.3 constant_dynamic-slice_fusion.6
  9.2 0.2 copy.50
  9.5 0.8 collective-permute-start
  10.3 0.1 copy.49
  10.4 0.1 copy.48
  10.5 0.2 copy.47
  10.7 0.1 select_reduce_fusion.1
  10.9 0.1 select_reduce_fusion
  11.0 3.0 fusion.21
  14.0 7.3 %maximum_select_fusion = bf16[1024,768]{0,1:T(8,128)(2,1)S(1)} fusion(bf16[512,768]{0,1:T(8,128)(2,1)S(1)} %collective-permute-done, bf16[512,128]{0,1:T(8,128)(2,1)S(1)} %copy.49, bf16[512,128]{0,1:T(8,128)(2,1)S(1)} %copy.48, bf16[512,512]{0,1:T(8,128)(2,1)S(1)} %copy.47, pred[]{:T(512)S(6)} %eq.12), kind=kLoop, calls=%fused_computation.18 | loop fusion | flops 13369344 | bytes 3145729 | tf_op jit(solution)/shard_map/jit(_where)/select_n | solution.py:140
  21.2 0.1 slice.28
  21.3 0.1 fusion.28
  21.5 0.9 copy-done
  22.4 1.4 copy.54
  23.8 1.4 copy.53
  25.2 2.7 fusion.4
  27.9 0.9 pad_maximum_fusion.3
  28.9 1.7 slice_bitcast_fusion
  30.6 0.2 all-gather.7.cloned.1.call-start
  30.8 0.5 slice.21
  33.9 0.2 multiply_convert_fusion
  34.1 0.3 tile.4
  34.4 1.3 copy.56
  35.9 3.0 convert_convert_fusion
  38.8 1.6 fusion.7
  40.4 1.6 copy.44
  42.0 1.5 pad_maximum_fusion.1.q_ref
  43.4 36.5 %all-gather.9.cloned.1.call-done = bf16[16384,1,128]{2,0,1:T(8,128)(2,1)} async-done(((bf16[1024,1,128]{2,0,1:T(8,128)(2,1)}), bf16[16384,1,128]{2,0,1:T(8,128)(2,1)}) %all-gather.9.cloned.1.call-update) | async-done | bytes 4194320 | tf_op jit(solution)/shard_map/all_gather | solution.py:151
  80.0 7.1 %pad_maximum_fusion.k_ref = bf16[16384,256]{1,0:T(8,128)(2,1)} fusion(bf16[16384,128]{1,0:T(8,128)(2,1)} %convert_convert_fusion, bf16[16384,128]{1,0:T(8,128)(2,1)} %bitcast.42), kind=kLoop, calls=%fused_computation | loop fusion | flops 16777216 | bytes 16777216 | tf_op jit(solution)/shard_map/concatenate | solution.py:154
  87.1 46.1 %all-gather.5.cloned.1.call-done.v_ref = bf16[2048,1024]{1,0:T(8,128)(2,1)} async-done(((bf16[128,1024]{1,0:T(8,128)(2,1)}), bf16[2048,1024]{1,0:T(8,128)(2,1)}) %all-gather.5.cloned.1.call-update) | async-done | bytes 4194320 | tf_op jit(solution)/shard_map/all_gather | solution.py:152
  133.3 71.2 %shard_map.55 = bf16[128,4096]{1,0:T(8,128)(2,1)S(1)} custom-call(s32[2]{0:T(128)S(1)} %pad_add_fusion.first_ref, bf16[256,4096]{1,0:T(8,128)(2,1)} %pad_maximum_fusion.1.q_ref, bf16[16384,256]{1,0:T(8,128)(2,1)} %pad_maximum_fusion.k_ref, bf16[2048,1024]{1,0:T(8,128)(2,1)} %all-gather.5.cloned.1.call-done.v_ref), custom_call_target="tpu_custom_call" | custom-call | tf_op jit(solution)/shard_map/pallas_call | solution.py:105
  204.6 1.3 copy.46
  206.0 9.0 %fusion.27 = (bf16[512,2048]{1,0:T(8,128)(2,1)S(1)}, bf16[512,2048]{1,0:T(8,128)(2,1)}, bf16[512,2048]{1,0:T(8,128)(2,1)}) fusion(bf16[1024,8192]{1,0:T(8,128)(2,1)} %param.9, s32[]{:T(128)S(6)} %select_n.117, s32[]{:T(128)S(6)} %select_n.131, s32[]{:T(128)S(6)} %select_n.124, s32[]{:T(128)S(6)} %select_n.128), kind=kLoop, calls=%fused_computation.60 | loop fusion | bytes 12582928 | tf_op jit(solution)/shard_map/dynamic_slice | solution.py:129
  215.0 2.9 collective-permute-start.2
  217.9 0.4 collective-permute-start.1
  218.3 2.3 collective-permute-start.3
  220.5 111.3 %all-gather.7.cloned.1.call-done = bf16[4,1024,512]{2,1,0:T(8,128)(2,1)} async-done(((bf16[1,1024,512]{2,1,0:T(8,128)(2,1)}), bf16[4,1024,512]{2,1,0:T(8,128)(2,1)}) %all-gather.7.cloned.1.call-update) | async-done | bytes 4194320 | tf_op jit(solution)/shard_map/all_gather | solution.py:159
  331.8 4.6 %fusion.5 = f32[1024,2048]{1,0:T(8,128)S(1)} fusion(bf16[1024,8192]{1,0:T(8,128)(2,1)} %param.9, s32[]{:T(128)S(6)} %select_n.117, s32[]{:T(128)S(6)} %select_n.119, bf16[4,1024,512]{2,1,0:T(8,128)(2,1)} %all-gather.7.cloned.1.call-done, s32[]{:T(128)S(6)} %select_n.116), kind=kOutput, calls=%fused_computation.16 | convolution fusion | flops 2147483648 | bytes 11534348 | tf_op jit(solution)/shard_map/dot_general | solution.py:164
  336.4 7.2 %fusion.12 = f32[1024,2048]{1,0:T(8,128)} fusion(bf16[512,2048]{1,0:T(8,128)(2,1)} %collective-permute-done.2, bf16[4,1024,512]{2,1,0:T(8,128)(2,1)S(1)} %copy-done.2, s32[]{:T(128)S(6)} %select_n.126), kind=kOutput, calls=%fused_computation.25 | convolution fusion | flops 2147483648 | bytes 11534340 | tf_op jit(solution)/shard_map/dot_general | solution.py:164
  343.6 7.2 %fusion.14 = f32[1024,2048]{1,0:T(8,128)} fusion(bf16[512,2048]{1,0:T(8,128)(2,1)} %collective-permute-done.1, bf16[4,1024,512]{2,1,0:T(8,128)(2,1)S(1)} %copy-done.2, s32[]{:T(128)S(6)} %select_n.121), kind=kOutput, calls=%fused_computation.27 | convolution fusion | flops 2147483648 | bytes 11534340 | tf_op jit(solution)/shard_map/dot_general | solution.py:164
  350.8 9.7 %add_add_fusion = f32[1024,2048]{1,0:T(8,128)S(1)} fusion(f32[1024,2048]{1,0:T(8,128)} %fusion.12, f32[1024,2048]{1,0:T(8,128)S(1)} %fusion.5, f32[1024,2048]{1,0:T(8,128)} %fusion.14, bf16[512,2048]{1,0:T(8,128)(2,1)} %collective-permute-done.3, bf16[4,1024,512]{2,1,0:T(8,128)(2,1)} %all-gather.7.cloned.1.call-done, s32[]{:T(128)S(6)} %select_n.129), kind=kOutput, calls=%fused_computation.1 | convolution fusion | flops 2153775104 | bytes 36700164 | tf_op jit(solution)/shard_map/dot_general | solution.py:164
  360.5 0.5 constant_dynamic-slice_fusion
  361.1 0.5 collective-permute-start.4
  361.6 6.8 %collective-permute-done.4 = f32[512,2048]{1,0:T(8,128)S(1)} collective-permute-done((f32[512,2048]{1,0:T(8,128)S(1)}, f32[512,2048]{1,0:T(8,128)S(1)}, u32[]{:S(2)}, u32[]{:S(2)}) %collective-permute-start.4) | collective-permute-done | bytes 4194336 | tf_op jit(solution)/shard_map/ppermute | solution.py:167
  368.4 2.0 add_convert_fusion
  (25 shorter events, 0.4 us)
Async XLA Ops:
  6.5 73.5 %all-gather.9.cloned.1.call-start = ((), (), s32[]{:S(2)}) async-start(), calls=%async_computation.2 | async-start | bytes 4456448 | tf_op jit(solution)/shard_map/all_gather | solution.py:151
  9.2 1.5 copy-start.3
  9.5 4.5 %collective-permute-start = (bf16[512,768]{0,1:T(8,128)(2,1)S(1)}, bf16[512,768]{0,1:T(8,128)(2,1)S(1)}, u32[]{:S(2)}, u32[]{:S(2)}) collective-permute-start(bf16[512,768]{0,1:T(8,128)(2,1)S(1)} %pad_maximum_fusion.2), channel_id=1, source_target_pairs={{0,4},{4,0},{8,12},{12,8},{16,20},{20,16},{24,28},{28,24},{32,36},... | collective-permute-start | bytes 2359304 | tf_op jit(solution)/shard_map/ppermute | solution.py:139
  21.2 1.1 copy-start
  28.8 104.5 %all-gather.5.cloned.1.call-start = ((), (), s32[]{:S(2)}) async-start(), calls=%async_computation | async-start | bytes 4456448 | tf_op jit(solution)/shard_map/all_gather | solution.py:152
  30.6 301.3 %all-gather.7.cloned.1.call-start = ((), (), s32[]{:S(2)}) async-start(), calls=%async_computation.1 | async-start | bytes 5242880 | tf_op jit(solution)/shard_map/all_gather | solution.py:159
  40.4 1.6 copy-start.1
  215.0 121.4 %collective-permute-start.2 = (bf16[512,2048]{1,0:T(8,128)(2,1)}, bf16[512,2048]{1,0:T(8,128)(2,1)}, u32[]{:S(2)}, u32[]{:S(2)}) collective-permute-start(bf16[512,2048]{1,0:T(8,128)(2,1)} %get-tuple-element.7), channel_id=1, source_target_pairs={{0,2},{1,3},{2,0},{3,1},{4,6},{5,7},{6,4},{7,5},{8,10},{9,11},{10,... | collective-permute-start | bytes 6291464 | tf_op jit(solution)/shard_map/ppermute | solution.py:135
  217.9 125.8 %collective-permute-start.1 = (bf16[512,2048]{1,0:T(8,128)(2,1)}, bf16[512,2048]{1,0:T(8,128)(2,1)}, u32[]{:S(2)}, u32[]{:S(2)}) collective-permute-start(bf16[512,2048]{1,0:T(8,128)(2,1)} %get-tuple-element.6), channel_id=1, source_target_pairs={{0,1},{1,2},{2,3},{3,0},{4,5},{5,6},{6,7},{7,4},{8,9},{9,10},{10,1... | collective-permute-start | bytes 6291464 | tf_op jit(solution)/shard_map/ppermute | solution.py:135
  218.3 132.6 %collective-permute-start.3 = (bf16[512,2048]{1,0:T(8,128)(2,1)S(1)}, bf16[512,2048]{1,0:T(8,128)(2,1)}, u32[]{:S(2)}, u32[]{:S(2)}) collective-permute-start(bf16[512,2048]{1,0:T(8,128)(2,1)S(1)} %get-tuple-element.5), channel_id=1, source_target_pairs={{0,3},{1,0},{2,1},{3,2},{4,7},{5,4},{6,5},{7,6},{8,11},{9,8},{10,9... | collective-permute-start | bytes 6291464 | tf_op jit(solution)/shard_map/ppermute | solution.py:135
  331.8 4.6 %copy-start.2 = (bf16[4,1024,512]{2,1,0:T(8,128)(2,1)S(1)}, bf16[4,1024,512]{2,1,0:T(8,128)(2,1)}, u32[]{:S(2)}) copy-start(bf16[4,1024,512]{2,1,0:T(8,128)(2,1)} %all-gather.7.cloned.1.call-done) | copy-start | bytes 12582916
  361.1 7.3 %collective-permute-start.4 = (f32[512,2048]{1,0:T(8,128)S(1)}, f32[512,2048]{1,0:T(8,128)S(1)}, u32[]{:S(2)}, u32[]{:S(2)}) collective-permute-start(f32[512,2048]{1,0:T(8,128)S(1)} %constant_dynamic-slice_fusion), channel_id=1, source_target_pairs={{0,4},{4,0},{8,12},{12,8},{16,20},{20,16},{24,28},{28,24},{32,36},... | collective-permute-start | bytes 12582920 | tf_op jit(solution)/shard_map/ppermute | solution.py:167
Sparse Core Ops, SparseCore 0:
  28.9 51.0 all-gather.8
  82.1 51.1 all-gather.4
  206.1 125.6 all-gather.6

commit v2 on v1

v2 whole, which is shorter than its diff:
```python
import math

import jax
import jax.numpy as jnp
from jax import lax
from jax.experimental import pallas as pl
from jax.experimental.pallas import tpu as pltpu
from jax.sharding import PartitionSpec as P

f32, bf16 = jnp.float32, jnp.bfloat16
rope_base = 1000000.0
ramp_low = 23.0
ramp_high = 40.0
yarn_factor = 4.0
mscale = 0.1 * math.log(4.0) + 1.0
neg_large = -1e30
exp2_scale = math.log2(math.e) / math.sqrt(128.0)
doc_penalty = 131072.0

NDOCS = 8
BLOCK = 1024
GROUP = 4
HALF = 512
CHUNK = 256
TILE = GROUP * CHUNK
CHUNKS = BLOCK // CHUNK
SLOTS = 9
OUTER = 6
MESH = pl.DeviceIdType.MESH


def doc_bounds(lengths):
    index = jnp.arange(NDOCS)
    ends = jnp.sum(jnp.where(index[None, :] <= index[:, None], lengths[None, :], 0), axis=1)
    return ends - lengths, ends


def inverse_frequencies():
    pair_index = jnp.arange(64).astype(f32)
    extrap = jnp.exp(-(2.0 * pair_index / 128.0) * math.log(rope_base))
    ramp = jnp.clip((pair_index - ramp_low) / (ramp_high - ramp_low), 0.0, 1.0)
    return extrap / yarn_factor * ramp + extrap * (1.0 - ramp)


def prepare_kernel(lengths, first_ref, inverse, queries, keys, values, q_ref, k_ref, v_ref):
    first = first_ref[0]
    lane = lax.broadcasted_iota(jnp.int32, (HALF, 128), 1)
    at = first + lax.broadcasted_iota(jnp.int32, (HALF, 128), 0)
    start = jnp.zeros((HALF, 128), jnp.int32)
    document = lax.broadcasted_iota(jnp.int32, (128, HALF), 0)
    across = first + lax.broadcasted_iota(jnp.int32, (128, HALF), 1)
    hidden = document < NDOCS
    end = 0
    for j in range(NDOCS):
        begin, end = end, end + lengths[j]
        start = start + jnp.where(at >= end, lengths[j], 0)
        hidden = hidden & ~((document == j) & (across >= begin) & (across < end))
    penalty = jnp.where(hidden, -doc_penalty, 0.0).astype(bf16)
    angles = (at - start).astype(f32) * inverse[...]
    cosine = jnp.cos(angles) * mscale
    sine = jnp.sin(angles) * mscale
    sine = jnp.where(lane < 64, -sine, sine)

    def rotated(ref, head):
        x = ref[:, head * 128 : (head + 1) * 128].astype(f32)
        return x * cosine + pltpu.roll(x, 64, 1) * sine

    for kv in range(2):
        for member in range(GROUP):
            turned = jnp.transpose(rotated(queries, kv * GROUP + member)).astype(bf16)
            for chunk in range(HALF // CHUNK):
                cols = slice(chunk * TILE + member * CHUNK, chunk * TILE + (member + 1) * CHUNK)
                tokens = slice(chunk * CHUNK, (chunk + 1) * CHUNK)
                q_ref[kv, 0:128, cols] = turned[:, tokens]
                q_ref[kv, 128:256, cols] = penalty[:, tokens]
        k_ref[kv] = rotated(keys, kv).astype(bf16)
        v_ref[kv] = jnp.transpose(values[:, kv * 128 : (kv + 1) * 128].astype(f32)).astype(bf16)


def prepare(lengths, first, queries, keys, values):
    inverse = inverse_frequencies()
    inverse = jnp.concatenate([inverse, inverse])[None, :]
    smem = pl.BlockSpec(memory_space=pltpu.SMEM)
    vmem = pl.BlockSpec(memory_space=pltpu.VMEM)
    return pl.pallas_call(
        prepare_kernel,
        out_shape=(
            jax.ShapeDtypeStruct((2, 256, GROUP * HALF), bf16),
            jax.ShapeDtypeStruct((2, HALF, 128), bf16),
            jax.ShapeDtypeStruct((2, 128, HALF), bf16),
        ),
        in_specs=[smem, smem, vmem, vmem, vmem, vmem],
        out_specs=(vmem, vmem, vmem),
        compiler_params=pltpu.CompilerParams(vmem_limit_bytes=40 * 2**20),
    )(lengths, first, inverse, queries, keys, values)


def main_kernel(
    bounds, qp, kp, vp, w_hbm, o_ref,
    q, kbuf, vbuf, top, total, acc, wbuf, att, given, taken,
    local_sem, swap_send, swap_recv, k_send, k_recv, v_send, v_recv,
    w_send, w_recv, c_send, c_recv, a_send, a_recv, p_send, p_recv,
):
    ctx = lax.axis_index("ctx")
    z = lax.axis_index("head")
    core = lax.rem(ctx, 2)
    chip = ctx // 2
    x = lax.rem(chip, 4)
    y = chip // 4
    other = 1 - core
    mate = (ctx + 1 - 2 * core, z)

    def at(x_, y_):
        return ((y_ * 4 + x_) * 2 + core, z)

    def remote(src, dst, send, recv, device):
        return pltpu.make_async_remote_copy(
            src_ref=src, dst_ref=dst, send_sem=send, recv_sem=recv, device_id=device, device_id_type=MESH
        )

    begin, end = bounds[0:1, :], bounds[1:2, :]
    for slot in range(SLOTS):
        where = (chip - slot) * BLOCK + lax.broadcasted_iota(jnp.int32, (BLOCK, 128), 0)
        kbuf[slot, :, 128:256] = jnp.where((where >= begin) & (where < end), 1.0, 0.0).astype(bf16)

    barrier = pltpu.get_barrier_semaphore()
    pl.semaphore_signal(barrier, inc=1, device_id=mate, device_id_type=MESH)
    for step in (1, 2, 3):
        for device in (
            at(lax.rem(x + step, 4), y),
            at(x, lax.rem(y + step, 4)),
            (ctx, lax.rem(z + step, 4)),
        ):
            pl.semaphore_signal(barrier, inc=1, device_id=device, device_id_type=MESH)
    pl.semaphore_wait(barrier, 10)

    mine = pl.ds(pl.multiple_of(core * HALF, HALF), HALF)
    mine_q = pl.ds(pl.multiple_of(core * GROUP * HALF, GROUP * HALF), GROUP * HALF)
    swaps = [
        remote(kp.at[other], kbuf.at[0, mine, pl.ds(0, 128)], swap_send.at[0], swap_recv.at[0], mate),
        remote(vp.at[other], vbuf.at[0, :, mine], swap_send.at[1], swap_recv.at[1], mate),
        remote(qp.at[other], q.at[:, mine_q], swap_send.at[2], swap_recv.at[2], mate),
    ]
    for copy in swaps:
        copy.start()
    rows = core * HALF

    def columns(s):
        return pl.ds(pl.multiple_of(lax.rem(z + s, 4) * 2048, 2048), 2048)

    piece = pl.ds(pl.multiple_of(y * 128, 128), 128)
    w_own = pltpu.make_async_copy(
        w_hbm.at[pl.ds(pl.multiple_of(rows, HALF), HALF), columns(0)], wbuf.at[0], local_sem.at[3]
    )
    w_piece = remote(
        w_hbm.at[pl.ds(pl.multiple_of(rows + y * 128, 128), 128), columns(2)],
        wbuf.at[2, piece, :], w_send.at[2], w_recv.at[2], (ctx, lax.rem(z + 2, 4)),
    )
    w_whole = [
        remote(
            w_hbm.at[pl.ds(pl.multiple_of(rows, HALF), HALF), columns(s)],
            wbuf.at[s], w_send.at[s], w_recv.at[s], (ctx, lax.rem(z + s, 4)),
        )
        for s in (1, 3)
    ]
    locals_ = [
        pltpu.make_async_copy(kp.at[core], kbuf.at[0, mine, pl.ds(0, 128)], local_sem.at[0]),
        pltpu.make_async_copy(vp.at[core], vbuf.at[0, :, mine], local_sem.at[1]),
        pltpu.make_async_copy(qp.at[core], q.at[:, mine_q], local_sem.at[2]),
    ]
    for copy in locals_:
        copy.start()
    w_piece.start()
    for copy in w_whole:
        copy.start()
    w_own.start()

    def share(slot, far, device, index):
        return (
            remote(kbuf.at[slot, :, pl.ds(0, 128)], kbuf.at[far, :, pl.ds(0, 128)], k_send.at[index], k_recv.at[far], device),
            remote(vbuf.at[slot], vbuf.at[far], v_send.at[index], v_recv.at[far], device),
        )

    down = [(y + s <= 3, share(0, 4 * s, at(x, lax.rem(y + s, 4)), s - 1)) for s in (1, 2)]
    row = []
    for s in (1, 2, 3):
        x_ = lax.rem(x + s, 4)
        row.append((x + s <= 3, share(0, s, at(x_, y), 1 + s)))
    second, third = [], []
    for s in (1, 2, 3):
        x_ = lax.rem(x + s, 4)
        second.append((y >= 1, share(4, 4 + x_ - x, at(x_, y), 4 + s)))
        third.append(((y >= 2) & (x_ < x), share(8, lax.rem(8 + x_ - x, 9), at(x_, y), 7 + s)))

    def go(list_):
        for condition, copies in list_:
            @pl.when(condition)
            def _():
                for copy in copies:
                    copy.start()

    def arrived(slot):
        for copy in share(slot, slot, mate, 0):
            copy.wait_recv()

    for copy in swaps[:2]:
        copy.wait_recv()
    for copy in locals_[:2]:
        copy.wait()
    go(down)
    go(row)
    swaps[2].wait_recv()
    locals_[2].wait()

    for chunk in range(CHUNKS):
        cols = slice(chunk * TILE, (chunk + 1) * TILE)
        seen = (chunk + 1) * CHUNK
        s = jnp.dot(kbuf[0, 0:seen, :], q[:, cols], preferred_element_type=f32)
        key = lax.broadcasted_iota(jnp.int32, s.shape, 0)
        query = chunk * CHUNK + lax.rem(lax.broadcasted_iota(jnp.int32, s.shape, 1), CHUNK)
        s = jnp.where(key <= query, s, neg_large)
        new = jnp.max(s, axis=0, keepdims=True)
        p = jnp.exp2((s - new) * exp2_scale)
        top[chunk] = new
        total[chunk] = jnp.sum(p, axis=0, keepdims=True)
        acc[chunk] = jnp.dot(vbuf[0, :, 0:seen], p.astype(bf16), preferred_element_type=f32)

    def add(slot, chunk):
        cols = pl.ds(pl.multiple_of(chunk * TILE, TILE), TILE)
        s = jnp.dot(kbuf[slot], q[:, cols], preferred_element_type=f32)
        old = top[chunk]
        new = jnp.maximum(old, jnp.max(s, axis=0, keepdims=True))
        p = jnp.exp2((s - new) * exp2_scale)
        scale = jnp.exp2((old - new) * exp2_scale)
        total[chunk] = total[chunk] * scale + jnp.sum(p, axis=0, keepdims=True)
        top[chunk] = new
        acc[chunk] = acc[chunk] * scale + jnp.dot(vbuf[slot], p.astype(bf16), preferred_element_type=f32)

    def slot_of(i):
        of_second = jnp.where(i < 4, i, i + 1)
        of_third = jnp.where(i == x + 4, 8, i)
        later = jnp.where(i == x, 4, jnp.where(i <= x + 3, of_second, of_third))
        return jnp.where(i < x, i + 1, later)

    def forward(slot, rows_before, list_):
        @pl.when(y >= rows_before)
        def _():
            arrived(slot)
        go(list_)

    c_copies = []
    for s in (1, 2, 3):
        y_ = lax.rem(y + s, 4)
        c_copies.append(
            remote(wbuf.at[2, piece, :], wbuf.at[2, piece, :], c_send.at[s - 1], c_recv.at[s - 1], at(x, y_))
        )

    def block_step(i, _):
        @pl.when(i == jnp.minimum(x, 1))
        def _():
            forward(4, 1, second)

        @pl.when(i == 3)
        def _():
            forward(8, 2, third)

        @pl.when(i == 4)
        def _():
            w_piece.wait_recv()
            for copy in c_copies:
                copy.start()

        slot = slot_of(i)

        @pl.when(chip >= slot)
        def _():
            @pl.when((slot != 4) & (slot != 8))
            def _():
                arrived(slot)

            def one(chunk, _):
                add(slot, chunk)
                return 0

            lax.fori_loop(0, CHUNKS, one, 0)

        return 0

    lax.fori_loop(0, OUTER, block_step, 0)
    for i in range(OUTER, 8):
        slot = slot_of(i)

        @pl.when((chip >= slot) & (slot != 4) & (slot != 8))
        def _():
            arrived(slot)

    def chunk_of(i):
        return lax.rem(i + 2 * other, CHUNKS)

    def sends(i):
        chunk = chunk_of(i)
        return [
            remote(att.at[i, 0], att.at[i, s], a_send.at[i, s], a_recv.at[i, s], (ctx, lax.rem(z + s, 4)))
            for s in (1, 2, 3)
        ]

    def finish(i, _):
        chunk = chunk_of(i)
        for j in range(OUTER, 8):
            slot = slot_of(j)

            @pl.when(chip >= slot)
            def _():
                add(slot, chunk)

        out = acc[chunk] / total[chunk]
        for member in range(GROUP):
            cols = slice(member * CHUNK, (member + 1) * CHUNK)
            att[i, 0, :, member * 128 : (member + 1) * 128] = jnp.transpose(out[:, cols]).astype(bf16)
        for copy in sends(i):
            copy.start()
        return 0

    lax.fori_loop(0, CHUNKS, finish, 0)

    w_own.wait()
    for copy in w_whole:
        copy.wait_recv()
    for s in (1, 2, 3):
        remote(
            wbuf.at[2, piece, :],
            wbuf.at[2, pl.ds(pl.multiple_of(lax.rem(y + 4 - s, 4) * 128, 128), 128), :],
            c_send.at[s - 1], c_recv.at[s - 1], mate,
        ).wait_recv()

    def exchange(i):
        return remote(given.at[i], taken.at[i], p_send.at[i], p_recv.at[i], mate)

    def project(i, keep):
        for copy in sends(i):
            copy.wait_recv()

        def some(n, _):
            cols = pl.ds(pl.multiple_of(n * 512, 512), 512)
            part = jnp.dot(att[i, 0], wbuf[0, :, cols], preferred_element_type=f32)
            for s in (1, 2, 3):
                part = part + jnp.dot(att[i, s], wbuf[s, :, cols], preferred_element_type=f32)
            keep(cols, part)
            return 0

        lax.fori_loop(0, 4, some, 0)

    for i in (0, 1):
        def give(cols, part):
            given[i, :, cols] = part

        project(i, give)
        exchange(i).start()
    for i in (0, 1):
        exchange(i).wait_recv()

        def keep(cols, part):
            o_ref[i * CHUNK : (i + 1) * CHUNK, cols] = (part + taken[i, :, cols]).astype(bf16)

        project(i + 2, keep)

    for copy in swaps + w_whole + [w_piece] + c_copies:
        copy.wait_send()
    for list_ in (down, row, second, third):
        for condition, copies in list_:
            @pl.when(condition)
            def _():
                for copy in copies:
                    copy.wait_send()
    for i in range(CHUNKS):
        for copy in sends(i):
            copy.wait_send()
    for i in (0, 1):
        exchange(i).wait_send()


def attend_and_project(bounds, q, k, v, out_weight):
    vmem = pl.BlockSpec(memory_space=pltpu.VMEM)
    dma = pltpu.SemaphoreType.DMA
    return pl.pallas_call(
        main_kernel,
        out_shape=jax.ShapeDtypeStruct((HALF, 2048), bf16),
        in_specs=[vmem, vmem, vmem, vmem, pl.BlockSpec(memory_space=pl.ANY)],
        out_specs=vmem,
        scratch_shapes=[
            pltpu.VMEM((256, GROUP * BLOCK), bf16),
            pltpu.VMEM((SLOTS, BLOCK, 256), bf16),
            pltpu.VMEM((SLOTS, 128, BLOCK), bf16),
            pltpu.VMEM((CHUNKS, 1, TILE), f32),
            pltpu.VMEM((CHUNKS, 1, TILE), f32),
            pltpu.VMEM((CHUNKS, 128, TILE), f32),
            pltpu.VMEM((4, HALF, 2048), bf16),
            pltpu.VMEM((CHUNKS, 4, CHUNK, 512), bf16),
            pltpu.VMEM((2, CHUNK, 2048), f32),
            pltpu.VMEM((2, CHUNK, 2048), f32),
            dma((4,)), dma((3,)), dma((3,)),
            dma((11,)), dma((SLOTS,)), dma((11,)), dma((SLOTS,)),
            dma((4,)), dma((4,)), dma((3,)), dma((3,)),
            dma((CHUNKS, 4)), dma((CHUNKS, 4)), dma((2,)), dma((2,)),
        ],
        compiler_params=pltpu.CompilerParams(
            collective_id=0, has_side_effects=True, vmem_limit_bytes=60 * 2**20
        ),
    )(bounds, q, k, v, out_weight)


def per_device(queries, keys, values, lengths, out_weight):
    device = lax.axis_index("ctx")
    starts, ends = doc_bounds(lengths)
    bounds = jnp.pad(jnp.stack([starts, ends]), ((0, 6), (0, 128 - NDOCS)))
    first = (device * HALF).astype(jnp.int32).reshape(1)
    q, k, v = prepare(lengths, first, queries, keys, values)
    return attend_and_project(bounds, q, k, v, out_weight)


def solution(mesh):
    return jax.shard_map(
        per_device,
        mesh=mesh,
        in_specs=(P("ctx", "head"), P("ctx", "head"), P("ctx", "head"), P(), P("head", None)),
        out_specs=P("ctx", "head"),
        check_vma=False,
    )
```

time: 377 us -> 157 us (0.42)
  the two profiles are of different devices: /device:TPU:31 before, /device:TPU:16 now
where the time goes in v2:
time: 157 us
  Pallas kernels  145 us (92%)
  local copies, waits for them, and re-layouts  10.3 us (7%)
    pallas_call x1, Pallas kernels, attend_and_project(): pl.pallas_call(main_kernel, out_shape=jax.ShapeDtypeStruct((HALF, 2048),...  142 us
    unnamed x15, local copies, waits for them, and re-layouts  9.66 us

profile of v2, /device:TPU:16, one launch (start us, length us, event | category | flops | bytes accessed | tf_op | source)
XLA Modules:
  0.0 156.8 jit_solution(16047271651387150332)
XLA Ops:
  0.0 0.8 select_reduce_fusion
  0.8 0.7 subtract_bitcast_fusion
  1.5 0.1 maximum_bitcast_fusion.inverse
  1.5 0.6 pad.4.bounds
  2.1 0.0 copy-start.1
  2.1 1.2 copy-done.1
  3.4 0.0 copy-start.4
  3.4 0.9 copy-done.4
  4.3 0.0 copy-start.5
  4.3 0.9 copy-done.5
  5.3 0.0 copy-start.6
  5.3 0.7 copy-done.6
  5.9 2.8 %shard_map.55 = (bf16[2,256,2048]{2,1,0:T(8,128)(2,1)S(1)}, bf16[2,512,128]{2,1,0:T(8,128)(2,1)S(1)}, bf16[2,128,512]{2,1,0:T(8,128)(2,1)S(1)}) custom-call(s32[8]{0:T(128)S(1)} %copy-done.6, s32[1]{0:T(128)} %bitcast.2.first_ref, f32[1,128]{1,0:T(1,128)S(1)} %maximum_bitcast_fusion.inverse, bf16[512,1024]{1,0:T(8,128)(2,1)S(1)} %copy-done.1, ...), custom_call_target="tpu_custom_call" | custom-call | tf_op jit(solution)/shard_map/pallas_call | solution.py:85
  8.8 0.0 copy-start
  8.8 1.3 copy-done
  10.1 0.0 copy-start.2
  10.1 0.7 copy-done.2
  10.8 0.0 copy-start.3
  10.8 0.7 copy-done.3
  11.5 142.1 %shard_map.56 = bf16[512,2048]{1,0:T(8,128)(2,1)} custom-call(s32[8,128]{1,0:T(8,128)} %pad.4.bounds, bf16[2,256,2048]{2,1,0:T(8,128)(2,1)} %copy-done, bf16[2,512,128]{2,1,0:T(8,128)(2,1)} %copy-done.2, bf16[2,128,512]{2,1,0:T(8,128)(2,1)} %copy-done.3, bf16[1024,8192]{1,0:T(8,128)(2,1)} %w_hbm.1), custom_call_target="tpu_custom_call" | custom-call | tf_op jit(solution)/shard_map/pallas_call | solution.py:385
  153.6 3.2 %copy.7 = bf16[512,2048]{1,0:T(8,128)(2,1)} copy(bf16[512,2048]{1,0:T(8,128)(2,1)} %shard_map.56) | data formatting | bytes 4194304
  (2 shorter events, 0.0 us)
Async XLA Ops:
  2.1 1.2 copy-start.1
  3.4 0.9 copy-start.4
  4.3 0.9 copy-start.5
  5.3 0.7 copy-start.6
  8.8 1.3 copy-start
  10.1 0.7 copy-start.2
  10.8 0.7 copy-start.3

commit v3 on v2

--- a/solution.py
+++ b/solution.py
@@ -25,7 +25,7 @@
 TILE = GROUP * CHUNK
 CHUNKS = BLOCK // CHUNK
 SLOTS = 9
-OUTER = 6
+LAST = 4
 MESH = pl.DeviceIdType.MESH
 
 
@@ -97,9 +97,9 @@
 
 def main_kernel(
     bounds, qp, kp, vp, w_hbm, o_ref,
-    q, kbuf, vbuf, top, total, acc, wbuf, att, given, taken,
+    q, kbuf, vbuf, top, total, acc, wbuf, att, given, taken, s_even, s_odd,
     local_sem, swap_send, swap_recv, k_send, k_recv, v_send, v_recv,
-    w_send, w_recv, c_send, c_recv, a_send, a_recv, p_send, p_recv,
+    w_send, w_recv, z_send, z_recv, c_send, c_recv, a_send, a_recv, p_send, p_recv,
 ):
     ctx = lax.axis_index("ctx")
     z = lax.axis_index("head")
@@ -119,7 +119,8 @@
         )
 
     begin, end = bounds[0:1, :], bounds[1:2, :]
-    for slot in range(SLOTS):
+
+    def mark(slot):
         where = (chip - slot) * BLOCK + lax.broadcasted_iota(jnp.int32, (BLOCK, 128), 0)
         kbuf[slot, :, 128:256] = jnp.where((where >= begin) & (where < end), 1.0, 0.0).astype(bf16)
 
@@ -143,26 +144,52 @@
     ]
     for copy in swaps:
         copy.start()
-    rows = core * HALF
-
-    def columns(s):
-        return pl.ds(pl.multiple_of(lax.rem(z + s, 4) * 2048, 2048), 2048)
-
-    piece = pl.ds(pl.multiple_of(y * 128, 128), 128)
-    w_own = pltpu.make_async_copy(
-        w_hbm.at[pl.ds(pl.multiple_of(rows, HALF), HALF), columns(0)], wbuf.at[0], local_sem.at[3]
-    )
-    w_piece = remote(
-        w_hbm.at[pl.ds(pl.multiple_of(rows + y * 128, 128), 128), columns(2)],
-        wbuf.at[2, piece, :], w_send.at[2], w_recv.at[2], (ctx, lax.rem(z + 2, 4)),
-    )
+    first_row = core * HALF
+
+    def from_hbm(t, row, count):
+        return w_hbm.at[
+            pl.ds(pl.multiple_of(first_row + row, 64), count),
+            pl.ds(pl.multiple_of(lax.rem(z + t, 4) * 2048, 2048), 2048),
+        ]
+
+    w_own = pltpu.make_async_copy(from_hbm(0, 0, HALF), wbuf.at[0], local_sem.at[3])
     w_whole = [
-        remote(
-            w_hbm.at[pl.ds(pl.multiple_of(rows, HALF), HALF), columns(s)],
-            wbuf.at[s], w_send.at[s], w_recv.at[s], (ctx, lax.rem(z + s, 4)),
+        remote(from_hbm(t, 0, 256), wbuf.at[t, pl.ds(0, 256), :], w_send.at[i], w_recv.at[i], (ctx, lax.rem(z + t, 4)))
+        for i, t in enumerate((1, 3))
+    ]
+
+    def piece_of(t, which):
+        size, base = (128, 0) if t == 2 else (64, 256)
+        return pl.ds(pl.multiple_of(base + which * size, 64), size)
+
+    def own_piece(t):
+        return y if t == 2 else x
+
+    w_pieces, w_spread, w_awaited = [], [], []
+    for i, t in enumerate((2, 1, 3)):
+        size, base = (128, 0) if t == 2 else (64, 256)
+        held = wbuf.at[t, piece_of(t, own_piece(t)), :]
+        w_pieces.append(
+            remote(
+                from_hbm(t, base + own_piece(t) * size, size), held,
+                z_send.at[i], z_recv.at[i], (ctx, lax.rem(z + t, 4)),
+            )
         )
-        for s in (1, 3)
-    ]
+        for step in (1, 2, 3):
+            to = lax.rem(own_piece(t) + step, 4)
+            device = at(x, to) if t == 2 else at(to, y)
+            w_spread.append(remote(held, held, c_send.at[i, step - 1], c_recv.at[i, step - 1], device))
+            came = lax.rem(own_piece(t) + 4 - step, 4)
+            w_awaited.append(
+                remote(held, wbuf.at[t, piece_of(t, came), :], c_send.at[i, step - 1], c_recv.at[i, step - 1], mate)
+            )
+
+    def spread_weights():
+        for copy in w_pieces:
+            copy.wait_recv()
+        for copy in w_spread:
+            copy.start()
+
     locals_ = [
         pltpu.make_async_copy(kp.at[core], kbuf.at[0, mine, pl.ds(0, 128)], local_sem.at[0]),
         pltpu.make_async_copy(vp.at[core], vbuf.at[0, :, mine], local_sem.at[1]),
@@ -170,10 +197,10 @@
     ]
     for copy in locals_:
         copy.start()
-    w_piece.start()
-    for copy in w_whole:
+    for copy in w_pieces + w_whole:
         copy.start()
     w_own.start()
+    mark(0)
 
     def share(slot, far, device, index):
         return (
@@ -181,34 +208,47 @@
             remote(vbuf.at[slot], vbuf.at[far], v_send.at[index], v_recv.at[far], device),
         )
 
-    down = [(y + s <= 3, share(0, 4 * s, at(x, lax.rem(y + s, 4)), s - 1)) for s in (1, 2)]
-    row = []
-    for s in (1, 2, 3):
-        x_ = lax.rem(x + s, 4)
-        row.append((x + s <= 3, share(0, s, at(x_, y), 1 + s)))
-    second, third = [], []
-    for s in (1, 2, 3):
-        x_ = lax.rem(x + s, 4)
-        second.append((y >= 1, share(4, 4 + x_ - x, at(x_, y), 4 + s)))
-        third.append(((y >= 2) & (x_ < x), share(8, lax.rem(8 + x_ - x, 9), at(x_, y), 7 + s)))
-
-    def go(list_):
-        for condition, copies in list_:
-            @pl.when(condition)
-            def _():
-                for copy in copies:
-                    copy.start()
+    below = at(x, lax.rem(y + 1, 4))
+    own = [(y <= 2, share(0, 4, below, 0))]
+    second = [((y >= 1) & (y <= 2), share(4, 8, below, 1))]
+    third = []
+    for step in (1, 3, 2):
+        x_ = lax.rem(x + step, 4)
+        near = step != 2
+        own.append((x_ > x, share(0, lax.rem(4 + x_ - x, 4), at(x_, y), 1 + step)))
+        second.append((y >= 1 if near else (y >= 1) & (x_ < x), share(4, 4 + x_ - x, at(x_, y), 4 + step)))
+        if near:
+            third.append(((y >= 2) & (x_ < x), share(8, lax.rem(8 + x_ - x, 9), at(x_, y), 7 + step)))
+    down = [((y <= 2) & (chip >= 2), share(2, 6, below, 9))]
+
+    def pass_on(list_, slot=None, rows_before=0):
+        for part in (0, 1):
+            if slot is not None:
+                @pl.when(y >= rows_before)
+                def _():
+                    share(slot, slot, mate, 0)[part].wait_recv()
+            for condition, copies in list_:
+                @pl.when(condition)
+                def _():
+                    copies[part].start()
 
     def arrived(slot):
-        for copy in share(slot, slot, mate, 0):
-            copy.wait_recv()
+        @pl.when((slot != 4) & (slot != 8))
+        def _():
+            for copy in share(slot, slot, mate, 0):
+                copy.wait_recv()
+
+        @pl.when(slot == 2)
+        def _():
+            pass_on(down)
 
     for copy in swaps[:2]:
         copy.wait_recv()
     for copy in locals_[:2]:
         copy.wait()
-    go(down)
-    go(row)
+    pass_on(own)
+    for slot in range(1, SLOTS):
+        mark(slot)
     swaps[2].wait_recv()
     locals_[2].wait()
 
@@ -225,9 +265,12 @@
         total[chunk] = jnp.sum(p, axis=0, keepdims=True)
         acc[chunk] = jnp.dot(vbuf[0, :, 0:seen], p.astype(bf16), preferred_element_type=f32)
 
-    def add(slot, chunk):
+    def scores(slot, chunk):
         cols = pl.ds(pl.multiple_of(chunk * TILE, TILE), TILE)
-        s = jnp.dot(kbuf[slot], q[:, cols], preferred_element_type=f32)
+        return jnp.dot(kbuf[slot], q[:, cols], preferred_element_type=f32)
+
+    def add(scores_ref, slot, chunk):
+        s = scores_ref[...]
         old = top[chunk]
         new = jnp.maximum(old, jnp.max(s, axis=0, keepdims=True))
         p = jnp.exp2((s - new) * exp2_scale)
@@ -242,102 +285,132 @@
         later = jnp.where(i == x, 4, jnp.where(i <= x + 3, of_second, of_third))
         return jnp.where(i < x, i + 1, later)
 
-    def forward(slot, rows_before, list_):
-        @pl.when(y >= rows_before)
-        def _():
-            arrived(slot)
-        go(list_)
-
-    c_copies = []
-    for s in (1, 2, 3):
-        y_ = lax.rem(y + s, 4)
-        c_copies.append(
-            remote(wbuf.at[2, piece, :], wbuf.at[2, piece, :], c_send.at[s - 1], c_recv.at[s - 1], at(x, y_))
-        )
-
-    def block_step(i, _):
-        @pl.when(i == jnp.minimum(x, 1))
-        def _():
-            forward(4, 1, second)
-
-        @pl.when(i == 3)
-        def _():
-            forward(8, 2, third)
-
-        @pl.when(i == 4)
-        def _():
-            w_piece.wait_recv()
-            for copy in c_copies:
-                copy.start()
-
-        slot = slot_of(i)
-
-        @pl.when(chip >= slot)
-        def _():
-            @pl.when((slot != 4) & (slot != 8))
-            def _():
-                arrived(slot)
-
-            def one(chunk, _):
-                add(slot, chunk)
-                return 0
-
-            lax.fori_loop(0, CHUNKS, one, 0)
-
-        return 0
-
-    lax.fori_loop(0, OUTER, block_step, 0)
-    for i in range(OUTER, 8):
-        slot = slot_of(i)
-
-        @pl.when((chip >= slot) & (slot != 4) & (slot != 8))
-        def _():
-            arrived(slot)
-
     def chunk_of(i):
         return lax.rem(i + 2 * other, CHUNKS)
 
     def sends(i):
+        return [
+            remote(att.at[i, 0], att.at[i, t], a_send.at[i, t], a_recv.at[i, t], (ctx, lax.rem(z + t, 4)))
+            for t in (1, 3)
+        ]
+
+    def relays(i):
+        copies = []
+        for t, half, index in ((1, 0, 0), (3, 1, 2)):
+            part = pl.ds(half * (CHUNK // 2), CHUNK // 2)
+            copies.append(
+                remote(
+                    att.at[i, t, part, :], att.at[i, 2, part, :],
+                    a_send.at[i, index], a_recv.at[i, index], (ctx, lax.rem(z + t, 4)),
+                )
+            )
+        return copies
+
+    def relay(i):
+        for copy in sends(i):
+            copy.wait_recv()
+        for copy in relays(i):
+            copy.start()
+
+    def finish(i):
         chunk = chunk_of(i)
-        return [
-            remote(att.at[i, 0], att.at[i, s], a_send.at[i, s], a_recv.at[i, s], (ctx, lax.rem(z + s, 4)))
-            for s in (1, 2, 3)
-        ]
-
-    def finish(i, _):
-        chunk = chunk_of(i)
-        for j in range(OUTER, 8):
-            slot = slot_of(j)
-
-            @pl.when(chip >= slot)
-            def _():
-                add(slot, chunk)
-
         out = acc[chunk] / total[chunk]
         for member in range(GROUP):
             cols = slice(member * CHUNK, (member + 1) * CHUNK)
             att[i, 0, :, member * 128 : (member + 1) * 128] = jnp.transpose(out[:, cols]).astype(bf16)
         for copy in sends(i):
             copy.start()
-        return 0
-
-    lax.fori_loop(0, CHUNKS, finish, 0)
-
+
+    pass_on(second, 4, 1)
+    blocks = jnp.minimum(8, chip)
+
+    @pl.when(blocks >= LAST)
+    def _():
+        arrived(slot_of(0))
+        s_even[...] = scores(slot_of(0), jnp.where(blocks > LAST, 0, chunk_of(0)))
+
+        def block_step(i, _):
+            slot, later = slot_of(i), slot_of(i + 1)
+
+            @pl.when(i == 1 + x // 2)
+            def _():
+                pass_on(third, 8, 2)
+
+            s_odd[...] = scores(slot, 1)
+            add(s_even, slot, 0)
+            s_even[...] = scores(slot, 2)
+            add(s_odd, slot, 1)
+            arrived(later)
+            s_odd[...] = scores(slot, 3)
+            add(s_even, slot, 2)
+            s_even[...] = scores(later, jnp.where(i + 1 < blocks - LAST, 0, chunk_of(0)))
+            add(s_odd, slot, 3)
+            return 0
+
+        lax.fori_loop(0, blocks - LAST, block_step, 0)
+        spread_weights()
+
+        def chunk_step(i, _):
+            chunk = chunk_of(i)
+            slots = [slot_of(blocks - LAST + j) for j in range(LAST)]
+
+            @pl.when(i >= 2)
+            def _():
+                relay(i - 2)
+
+            for j in range(LAST):
+                ready, coming = (s_even, s_odd) if j % 2 == 0 else (s_odd, s_even)
+                if j + 1 < LAST:
+                    @pl.when(i == 0)
+                    def _():
+                        arrived(slots[j + 1])
+
+                    coming[...] = scores(slots[j + 1], chunk)
+                else:
+                    coming[...] = scores(slots[0], chunk_of(i + 1))
+                add(ready, slots[j], chunk)
+            finish(i)
+            return 0
+
+        lax.fori_loop(0, CHUNKS, chunk_step, 0)
+
+    @pl.when(blocks < LAST)
+    def _():
+        def block_here(j, _):
+            arrived(slot_of(j))
+            return 0
+
+        lax.fori_loop(0, blocks, block_here, 0)
+        spread_weights()
+
+        def chunk_step(i, _):
+            def one(j, _):
+                s_even[...] = scores(slot_of(j), chunk_of(i))
+                add(s_even, slot_of(j), chunk_of(i))
+                return 0
+
+            @pl.when(i >= 2)
+            def _():
+                relay(i - 2)
+
+            lax.fori_loop(0, blocks, one, 0)
+            finish(i)
+            return 0
+
+        lax.fori_loop(0, CHUNKS, chunk_step, 0)
+
+    relay(2)
     w_own.wait()
     for copy in w_whole:
         copy.wait_recv()
-    for s in (1, 2, 3):
-        remote(
-            wbuf.at[2, piece, :],
-            wbuf.at[2, pl.ds(pl.multiple_of(lax.rem(y + 4 - s, 4) * 128, 128), 128), :],
-            c_send.at[s - 1], c_recv.at[s - 1], mate,
-        ).wait_recv()
+    for copy in w_awaited:
+        copy.wait_recv()
 
     def exchange(i):
         return remote(given.at[i], taken.at[i], p_send.at[i], p_recv.at[i], mate)
 
     def project(i, keep):
-        for copy in sends(i):
+        for copy in relays(i):
             copy.wait_recv()
 
         def some(n, _):
@@ -356,6 +429,8 @@
 
         project(i, give)
         exchange(i).start()
+        if i == 0:
+            relay(3)
     for i in (0, 1):
         exchange(i).wait_recv()
 
@@ -364,16 +439,16 @@
 
         project(i + 2, keep)
 
-    for copy in swaps + w_whole + [w_piece] + c_copies:
+    for copy in swaps + w_whole + w_pieces + w_spread:
         copy.wait_send()
-    for list_ in (down, row, second, third):
+    for list_ in (own, second, third, down):
         for condition, copies in list_:
             @pl.when(condition)
             def _():
                 for copy in copies:
                     copy.wait_send()
     for i in range(CHUNKS):
-        for copy in sends(i):
+        for copy in sends(i) + relays(i):
             copy.wait_send()
     for i in (0, 1):
         exchange(i).wait_send()
@@ -398,9 +473,11 @@
             pltpu.VMEM((CHUNKS, 4, CHUNK, 512), bf16),
             pltpu.VMEM((2, CHUNK, 2048), f32),
             pltpu.VMEM((2, CHUNK, 2048), f32),
+            pltpu.VMEM((BLOCK, TILE), f32),
+            pltpu.VMEM((BLOCK, TILE), f32),
             dma((4,)), dma((3,)), dma((3,)),
             dma((11,)), dma((SLOTS,)), dma((11,)), dma((SLOTS,)),
-            dma((4,)), dma((4,)), dma((3,)), dma((3,)),
+            dma((2,)), dma((2,)), dma((3,)), dma((3,)), dma((3, 3)), dma((3, 3)),
             dma((CHUNKS, 4)), dma((CHUNKS, 4)), dma((2,)), dma((2,)),
         ],
         compiler_params=pltpu.CompilerParams(

time: 157 us -> 130 us (0.83)
  the two profiles are of different devices: /device:TPU:16 before, /device:TPU:19 now
where the time goes in v3:
time: 130 us
  Pallas kernels  118 us (91%)
  local copies, waits for them, and re-layouts  10.3 us (8%)
  other arithmetic  1.53 us (1%)
    pallas_call x1, Pallas kernels, attend_and_project(): pl.pallas_call(main_kernel, out_shape=jax.ShapeDtypeStruct((HALF, 2048),...  115 us
    unnamed x15, local copies, waits for them, and re-layouts  9.66 us
    pallas_call x1, Pallas kernels, prepare(): pl.pallas_call(prepare_kernel, out_shape=(jax.ShapeDtypeStruct((2, 256, G...  2.83 us

profile of v3, /device:TPU:19, one launch (start us, length us, event | category | flops | bytes accessed | tf_op | source)
XLA Modules:
  0.0 130.1 jit_solution(8519338421032955322)
XLA Ops:
  0.0 0.8 select_reduce_fusion
  0.8 0.7 subtract_bitcast_fusion
  1.5 0.1 maximum_bitcast_fusion.inverse
  1.5 0.6 pad.4.bounds
  2.1 0.0 copy-start.1
  2.1 1.2 copy-done.1
  3.4 0.0 copy-start.4
  3.4 0.9 copy-done.4
  4.3 0.0 copy-start.5
  4.3 0.9 copy-done.5
  5.3 0.0 copy-start.6
  5.3 0.7 copy-done.6
  5.9 2.8 %shard_map.55 = (bf16[2,256,2048]{2,1,0:T(8,128)(2,1)S(1)}, bf16[2,512,128]{2,1,0:T(8,128)(2,1)S(1)}, bf16[2,128,512]{2,1,0:T(8,128)(2,1)S(1)}) custom-call(s32[8]{0:T(128)S(1)} %copy-done.6, s32[1]{0:T(128)} %bitcast.2.first_ref, f32[1,128]{1,0:T(1,128)S(1)} %maximum_bitcast_fusion.inverse, bf16[512,1024]{1,0:T(8,128)(2,1)S(1)} %copy-done.1, ...), custom_call_target="tpu_custom_call" | custom-call | tf_op jit(solution)/shard_map/pallas_call | solution.py:85
  8.8 0.0 copy-start
  8.8 1.3 %copy-done = bf16[2,256,2048]{2,1,0:T(8,128)(2,1)} copy-done((bf16[2,256,2048]{2,1,0:T(8,128)(2,1)}, bf16[2,256,2048]{2,1,0:T(8,128)(2,1)S(1)}, u32[]{:S(2)}) %copy-start) | copy-done | bytes 2097176
  10.1 0.0 copy-start.2
  10.1 0.7 copy-done.2
  10.8 0.0 copy-start.3
  10.8 0.7 copy-done.3
  11.5 115.4 %shard_map.56 = bf16[512,2048]{1,0:T(8,128)(2,1)} custom-call(s32[8,128]{1,0:T(8,128)} %pad.4.bounds, bf16[2,256,2048]{2,1,0:T(8,128)(2,1)} %copy-done, bf16[2,512,128]{2,1,0:T(8,128)(2,1)} %copy-done.2, bf16[2,128,512]{2,1,0:T(8,128)(2,1)} %copy-done.3, bf16[1024,8192]{1,0:T(8,128)(2,1)} %w_hbm.1), custom_call_target="tpu_custom_call" | custom-call | tf_op jit(solution)/shard_map/pallas_call | solution.py:460
  126.9 3.2 %copy.7 = bf16[512,2048]{1,0:T(8,128)(2,1)} copy(bf16[512,2048]{1,0:T(8,128)(2,1)} %shard_map.56) | data formatting | bytes 4194304
  (2 shorter events, 0.0 us)
Async XLA Ops:
  2.1 1.2 copy-start.1
  3.4 0.9 copy-start.4
  4.3 0.9 copy-start.5
  5.3 0.7 copy-start.6
  8.8 1.3 %copy-start = (bf16[2,256,2048]{2,1,0:T(8,128)(2,1)}, bf16[2,256,2048]{2,1,0:T(8,128)(2,1)S(1)}, u32[]{:S(2)}) copy-start(bf16[2,256,2048]{2,1,0:T(8,128)(2,1)S(1)} %get-tuple-element.8.qp) | copy-start | bytes 6291460
  10.1 0.7 copy-start.2
  10.8 0.7 copy-start.3

commit v4 on v3

--- a/solution.py
+++ b/solution.py
@@ -29,12 +29,6 @@
 MESH = pl.DeviceIdType.MESH
 
 
-def doc_bounds(lengths):
-    index = jnp.arange(NDOCS)
-    ends = jnp.sum(jnp.where(index[None, :] <= index[:, None], lengths[None, :], 0), axis=1)
-    return ends - lengths, ends
-
-
 def inverse_frequencies():
     pair_index = jnp.arange(64).astype(f32)
     extrap = jnp.exp(-(2.0 * pair_index / 128.0) * math.log(rope_base))
@@ -42,19 +36,25 @@
     return extrap / yarn_factor * ramp + extrap * (1.0 - ramp)
 
 
-def prepare_kernel(lengths, first_ref, inverse, queries, keys, values, q_ref, k_ref, v_ref):
-    first = first_ref[0]
-    lane = lax.broadcasted_iota(jnp.int32, (HALF, 128), 1)
-    at = first + lax.broadcasted_iota(jnp.int32, (HALF, 128), 0)
-    start = jnp.zeros((HALF, 128), jnp.int32)
-    document = lax.broadcasted_iota(jnp.int32, (128, HALF), 0)
-    across = first + lax.broadcasted_iota(jnp.int32, (128, HALF), 1)
+def prepare_kernel(lengths, first_ref, inverse, queries, keys, values, q_ref, k_ref, v_ref, bounds_ref):
+    first = first_ref[0] + pl.program_id(0) * CHUNK
+    lane = lax.broadcasted_iota(jnp.int32, (CHUNK, 128), 1)
+    at = first + lax.broadcasted_iota(jnp.int32, (CHUNK, 128), 0)
+    start = jnp.zeros((CHUNK, 128), jnp.int32)
+    document = lax.broadcasted_iota(jnp.int32, (128, CHUNK), 0)
+    across = first + lax.broadcasted_iota(jnp.int32, (128, CHUNK), 1)
     hidden = document < NDOCS
+    bound_row = lax.broadcasted_iota(jnp.int32, (8, 128), 0)
+    bound_lane = lax.broadcasted_iota(jnp.int32, (8, 128), 1)
+    bounds = jnp.zeros((8, 128), jnp.int32)
     end = 0
     for j in range(NDOCS):
         begin, end = end, end + lengths[j]
         start = start + jnp.where(at >= end, lengths[j], 0)
         hidden = hidden & ~((document == j) & (across >= begin) & (across < end))
+        bounds = jnp.where((bound_lane == j) & (bound_row == 0), begin, bounds)
+        bounds = jnp.where((bound_lane == j) & (bound_row == 1), end, bounds)
+    bounds_ref[...] = bounds
     penalty = jnp.where(hidden, -doc_penalty, 0.0).astype(bf16)
     angles = (at - start).astype(f32) * inverse[...]
     cosine = jnp.cos(angles) * mscale
@@ -67,12 +67,9 @@
 
     for kv in range(2):
         for member in range(GROUP):
-            turned = jnp.transpose(rotated(queries, kv * GROUP + member)).astype(bf16)
-            for chunk in range(HALF // CHUNK):
-                cols = slice(chunk * TILE + member * CHUNK, chunk * TILE + (member + 1) * CHUNK)
-                tokens = slice(chunk * CHUNK, (chunk + 1) * CHUNK)
-                q_ref[kv, 0:128, cols] = turned[:, tokens]
-                q_ref[kv, 128:256, cols] = penalty[:, tokens]
+            cols = slice(member * CHUNK, (member + 1) * CHUNK)
+            q_ref[kv, 0:128, cols] = jnp.transpose(rotated(queries, kv * GROUP + member)).astype(bf16)
+            q_ref[kv, 128:256, cols] = penalty
         k_ref[kv] = rotated(keys, kv).astype(bf16)
         v_ref[kv] = jnp.transpose(values[:, kv * 128 : (kv + 1) * 128].astype(f32)).astype(bf16)
 
@@ -81,17 +78,30 @@
     inverse = inverse_frequencies()
     inverse = jnp.concatenate([inverse, inverse])[None, :]
     smem = pl.BlockSpec(memory_space=pltpu.SMEM)
-    vmem = pl.BlockSpec(memory_space=pltpu.VMEM)
     return pl.pallas_call(
         prepare_kernel,
+        grid=(HALF // CHUNK,),
         out_shape=(
             jax.ShapeDtypeStruct((2, 256, GROUP * HALF), bf16),
             jax.ShapeDtypeStruct((2, HALF, 128), bf16),
             jax.ShapeDtypeStruct((2, 128, HALF), bf16),
+            jax.ShapeDtypeStruct((8, 128), jnp.int32),
         ),
-        in_specs=[smem, smem, vmem, vmem, vmem, vmem],
-        out_specs=(vmem, vmem, vmem),
-        compiler_params=pltpu.CompilerParams(vmem_limit_bytes=40 * 2**20),
+        in_specs=[
+            smem,
+            smem,
+            pl.BlockSpec((1, 128), lambda i: (0, 0)),
+            pl.BlockSpec((CHUNK, 1024), lambda i: (i, 0)),
+            pl.BlockSpec((CHUNK, 256), lambda i: (i, 0)),
+            pl.BlockSpec((CHUNK, 256), lambda i: (i, 0)),
+        ],
+        out_specs=(
+            pl.BlockSpec((2, 256, TILE), lambda i: (0, 0, i)),
+            pl.BlockSpec((2, CHUNK, 128), lambda i: (0, i, 0)),
+            pl.BlockSpec((2, 128, CHUNK), lambda i: (0, 0, i)),
+            pl.BlockSpec((8, 128), lambda i: (0, 0)),
+        ),
+        compiler_params=pltpu.CompilerParams(vmem_limit_bytes=62 * 2**20),
     )(lengths, first, inverse, queries, keys, values)
 
 
@@ -242,6 +252,10 @@
         def _():
             pass_on(down)
 
+        @pl.when(slot == 8)
+        def _():
+            pass_on(third, 8, 2)
+
     for copy in swaps[:2]:
         copy.wait_recv()
     for copy in locals_[:2]:
@@ -280,10 +294,12 @@
         acc[chunk] = acc[chunk] * scale + jnp.dot(vbuf[slot], p.astype(bf16), preferred_element_type=f32)
 
     def slot_of(i):
-        of_second = jnp.where(i < 4, i, i + 1)
-        of_third = jnp.where(i == x + 4, 8, i)
-        later = jnp.where(i == x, 4, jnp.where(i <= x + 3, of_second, of_third))
-        return jnp.where(i < x, i + 1, later)
+        shift = jnp.where(y >= 2, 1, 0)
+        j = i - shift
+        of_second = jnp.where(j < 4, j, j + 1)
+        rest = jnp.where(j <= x + 3, of_second, i)
+        column = jnp.where(i == x, 4, jnp.where((y >= 2) & (i == x + 1), 8, rest))
+        return jnp.where(i < x, i + 1, column)
 
     def chunk_of(i):
         return lax.rem(i + 2 * other, CHUNKS)
@@ -332,10 +348,6 @@
         def block_step(i, _):
             slot, later = slot_of(i), slot_of(i + 1)
 
-            @pl.when(i == 1 + x // 2)
-            def _():
-                pass_on(third, 8, 2)
-
             s_odd[...] = scores(slot, 1)
             add(s_even, slot, 0)
             s_even[...] = scores(slot, 2)
@@ -348,11 +360,14 @@
             return 0
 
         lax.fori_loop(0, blocks - LAST, block_step, 0)
-        spread_weights()
 
         def chunk_step(i, _):
             chunk = chunk_of(i)
             slots = [slot_of(blocks - LAST + j) for j in range(LAST)]
+
+            @pl.when(i == 1)
+            def _():
+                spread_weights()
 
             @pl.when(i >= 2)
             def _():
@@ -381,13 +396,16 @@
             return 0
 
         lax.fori_loop(0, blocks, block_here, 0)
-        spread_weights()
 
         def chunk_step(i, _):
             def one(j, _):
                 s_even[...] = scores(slot_of(j), chunk_of(i))
                 add(s_even, slot_of(j), chunk_of(i))
                 return 0
+
+            @pl.when(i == 1)
+            def _():
+                spread_weights()
 
             @pl.when(i >= 2)
             def _():
@@ -460,7 +478,7 @@
     return pl.pallas_call(
         main_kernel,
         out_shape=jax.ShapeDtypeStruct((HALF, 2048), bf16),
-        in_specs=[vmem, vmem, vmem, vmem, pl.BlockSpec(memory_space=pl.ANY)],
+        in_specs=[vmem] + [pl.BlockSpec(memory_space=pl.ANY)] * 4,
         out_specs=vmem,
         scratch_shapes=[
             pltpu.VMEM((256, GROUP * BLOCK), bf16),
@@ -488,10 +506,8 @@
 
 def per_device(queries, keys, values, lengths, out_weight):
     device = lax.axis_index("ctx")
-    starts, ends = doc_bounds(lengths)
-    bounds = jnp.pad(jnp.stack([starts, ends]), ((0, 6), (0, 128 - NDOCS)))
     first = (device * HALF).astype(jnp.int32).reshape(1)
-    q, k, v = prepare(lengths, first, queries, keys, values)
+    q, k, v, bounds = prepare(lengths, first, queries, keys, values)
     return attend_and_project(bounds, q, k, v, out_weight)
 
 

time: 130 us -> 119 us (0.915)
  local copies, waits for them, and re-layouts: 10.3 us -> 3.16 us
  Pallas kernels: 118 us -> 115 us
    unnamed x15 -> x1, local copies, waits for them, and re-layouts: 9.66 us -> 3.16 us
    pallas_call x1, Pallas kernels: 115 us -> 110 us  [attend_and_project(): pl.pallas_call(main_kernel, out_shape=jax.ShapeDtypeStruct((HALF, 2048),...]
    pallas_call x1, Pallas kernels: 2.83 us -> 4.59 us  [prepare(): pl.pallas_call(prepare_kernel, grid=(HALF // CHUNK,), out_shape=(jax.Shap...]
where the time goes in v4:
time: 119 us
  Pallas kernels  115 us (97%)
  local copies, waits for them, and re-layouts  3.16 us (3%)
    pallas_call x1, Pallas kernels, attend_and_project(): pl.pallas_call(main_kernel, out_shape=jax.ShapeDtypeStruct((HALF, 2048),...  110 us
    pallas_call x1, Pallas kernels, prepare(): pl.pallas_call(prepare_kernel, grid=(HALF // CHUNK,), out_shape=(jax.Shap...  4.59 us
    unnamed x1, local copies, waits for them, and re-layouts  3.16 us

profile of v4, /device:TPU:19, one launch (start us, length us, event | category | flops | bytes accessed | tf_op | source)
XLA Modules:
  0.0 118.9 jit_solution(14313251931475973718)
XLA Ops:
  0.0 0.6 maximum_bitcast_fusion.inverse
  0.6 4.6 %shard_map.55 = (bf16[2,256,2048]{2,1,0:T(8,128)(2,1)}, bf16[2,512,128]{2,1,0:T(8,128)(2,1)}, bf16[2,128,512]{2,1,0:T(8,128)(2,1)}, s32[8,128]{1,0:T(8,128)}) custom-call(s32[8]{0:T(128)} %lengths.1, s32[1]{0:T(128)} %bitcast.first_ref, f32[1,128]{1,0:T(1,128)} %maximum_bitcast_fusion.inverse, bf16[512,1024]{1,0:T(8,128)(2,1)} %queries.1, ...), custom_call_target="tpu_custom_call" | custom-call | tf_op jit(solution)/shard_map/pallas_call | solution.py:81
  5.2 110.5 %shard_map.56 = bf16[512,2048]{1,0:T(8,128)(2,1)} custom-call(s32[8,128]{1,0:T(8,128)} %get-tuple-element.9.bounds, bf16[2,256,2048]{2,1,0:T(8,128)(2,1)} %get-tuple-element.10.qp, bf16[2,512,128]{2,1,0:T(8,128)(2,1)} %get-tuple-element.11.kp, bf16[2,128,512]{2,1,0:T(8,128)(2,1)} %get-tuple-element.12.vp, bf16[1024,8192]{1,0:T(8,128)(2,1)} %w_hbm.1), custom_call_target="tpu_custom_call" | custom-call | tf_op jit(solution)/shard_map/pallas_call | solution.py:478
  115.7 3.2 %copy.7 = bf16[512,2048]{1,0:T(8,128)(2,1)} copy(bf16[512,2048]{1,0:T(8,128)(2,1)} %shard_map.56) | data formatting | bytes 4194304
  (1 shorter events, 0.0 us)

commit v5 on v4

--- a/solution.py
+++ b/solution.py
@@ -185,9 +185,9 @@
                 z_send.at[i], z_recv.at[i], (ctx, lax.rem(z + t, 4)),
             )
         )
-        for step in (1, 2, 3):
+        for step in (1, 2, 3) if t != 2 else ():
             to = lax.rem(own_piece(t) + step, 4)
-            device = at(x, to) if t == 2 else at(to, y)
+            device = at(to, y)
             w_spread.append(remote(held, held, c_send.at[i, step - 1], c_recv.at[i, step - 1], device))
             came = lax.rem(own_piece(t) + 4 - step, 4)
             w_awaited.append(
@@ -195,10 +195,22 @@
             )
 
     def spread_weights():
-        for copy in w_pieces:
+        for copy in w_pieces[1:]:
             copy.wait_recv()
         for copy in w_spread:
             copy.start()
+
+    def down_y(k):
+        held = wbuf.at[2, piece_of(2, lax.rem(y + k, 4)), :]
+        return remote(held, held, c_send.at[0, k], c_recv.at[0, k], at(x, lax.rem(y + 3, 4)))
+
+    def from_up_y(k):
+        held = wbuf.at[2, piece_of(2, lax.rem(y + k + 1, 4)), :]
+        return remote(held, held, c_send.at[0, k], c_recv.at[0, k], mate)
+
+    def hand_on(k):
+        (from_up_y(k - 1) if k else w_pieces[0]).wait_recv()
+        down_y(k).start()
 
     locals_ = [
         pltpu.make_async_copy(kp.at[core], kbuf.at[0, mine, pl.ds(0, 128)], local_sem.at[0]),
@@ -338,6 +350,7 @@
             copy.start()
 
     pass_on(second, 4, 1)
+    hand_on(0)
     blocks = jnp.minimum(8, chip)
 
     @pl.when(blocks >= LAST)
@@ -365,9 +378,14 @@
             chunk = chunk_of(i)
             slots = [slot_of(blocks - LAST + j) for j in range(LAST)]
 
+            @pl.when(i == 0)
+            def _():
+                hand_on(1)
+
             @pl.when(i == 1)
             def _():
                 spread_weights()
+                hand_on(2)
 
             @pl.when(i >= 2)
             def _():
@@ -403,9 +421,14 @@
                 add(s_even, slot_of(j), chunk_of(i))
                 return 0
 
+            @pl.when(i == 0)
+            def _():
+                hand_on(1)
+
             @pl.when(i == 1)
             def _():
                 spread_weights()
+                hand_on(2)
 
             @pl.when(i >= 2)
             def _():
@@ -421,7 +444,7 @@
     w_own.wait()
     for copy in w_whole:
         copy.wait_recv()
-    for copy in w_awaited:
+    for copy in w_awaited + [from_up_y(2)]:
         copy.wait_recv()
 
     def exchange(i):
@@ -457,7 +480,7 @@
 
         project(i + 2, keep)
 
-    for copy in swaps + w_whole + w_pieces + w_spread:
+    for copy in swaps + w_whole + w_pieces + w_spread + [down_y(k) for k in range(3)]:
         copy.wait_send()
     for list_ in (own, second, third, down):
         for condition, copies in list_:

time: 119 us -> 117 us (0.983)
  the two profiles are of different devices: /device:TPU:19 before, /device:TPU:16 now
where the time goes in v5:
time: 117 us; the launch traced here: 116 us
  Pallas kernels  112 us (96%)
  local copies, waits for them, and re-layouts  3.16 us (3%)
    pallas_call x1, Pallas kernels, attend_and_project(): pl.pallas_call(main_kernel, out_shape=jax.ShapeDtypeStruct((HALF, 2048),...  107 us
    pallas_call x1, Pallas kernels, prepare(): pl.pallas_call(prepare_kernel, grid=(HALF // CHUNK,), out_shape=(jax.Shap...  4.59 us
    unnamed x1, local copies, waits for them, and re-layouts  3.16 us

profile of v5, /device:TPU:16, one launch (start us, length us, event | category | flops | bytes accessed | tf_op | source)
XLA Modules:
  0.0 115.7 jit_solution(7066658565719326930)
XLA Ops:
  0.0 0.6 maximum_bitcast_fusion.inverse
  0.6 4.6 %shard_map.55 = (bf16[2,256,2048]{2,1,0:T(8,128)(2,1)}, bf16[2,512,128]{2,1,0:T(8,128)(2,1)}, bf16[2,128,512]{2,1,0:T(8,128)(2,1)}, s32[8,128]{1,0:T(8,128)}) custom-call(s32[8]{0:T(128)} %lengths.1, s32[1]{0:T(128)} %bitcast.first_ref, f32[1,128]{1,0:T(1,128)} %maximum_bitcast_fusion.inverse, bf16[512,1024]{1,0:T(8,128)(2,1)} %queries.1, ...), custom_call_target="tpu_custom_call" | custom-call | tf_op jit(solution)/shard_map/pallas_call | solution.py:81
  5.2 107.3 %shard_map.56 = bf16[512,2048]{1,0:T(8,128)(2,1)} custom-call(s32[8,128]{1,0:T(8,128)} %get-tuple-element.9.bounds, bf16[2,256,2048]{2,1,0:T(8,128)(2,1)} %get-tuple-element.10.qp, bf16[2,512,128]{2,1,0:T(8,128)(2,1)} %get-tuple-element.11.kp, bf16[2,128,512]{2,1,0:T(8,128)(2,1)} %get-tuple-element.12.vp, bf16[1024,8192]{1,0:T(8,128)(2,1)} %w_hbm.1), custom_call_target="tpu_custom_call" | custom-call | tf_op jit(solution)/shard_map/pallas_call | solution.py:501
  112.5 3.2 %copy.7 = bf16[512,2048]{1,0:T(8,128)(2,1)} copy(bf16[512,2048]{1,0:T(8,128)(2,1)} %shard_map.56) | data formatting | bytes 4194304
  (1 shorter events, 0.0 us)

commit v6 on v5

--- a/solution.py
+++ b/solution.py
@@ -381,10 +381,10 @@
             @pl.when(i == 0)
             def _():
                 hand_on(1)
+                spread_weights()
 
             @pl.when(i == 1)
             def _():
-                spread_weights()
                 hand_on(2)
 
             @pl.when(i >= 2)
@@ -424,10 +424,10 @@
             @pl.when(i == 0)
             def _():
                 hand_on(1)
+                spread_weights()
 
             @pl.when(i == 1)
             def _():
-                spread_weights()
                 hand_on(2)
 
             @pl.when(i >= 2)

time: 117 us -> 117 us (level)
  no operation moved by 1% of the time
where the time goes in v6:
time: 117 us; the launch traced here: 116 us
  Pallas kernels  112 us (96%)
  local copies, waits for them, and re-layouts  3.16 us (3%)
    pallas_call x1, Pallas kernels, attend_and_project(): pl.pallas_call(main_kernel, out_shape=jax.ShapeDtypeStruct((HALF, 2048),...  107 us
    pallas_call x1, Pallas kernels, prepare(): pl.pallas_call(prepare_kernel, grid=(HALF // CHUNK,), out_shape=(jax.Shap...  4.59 us
    unnamed x1, local copies, waits for them, and re-layouts  3.16 us

profile of v6, /device:TPU:16, one launch (start us, length us, event | category | flops | bytes accessed | tf_op | source)
XLA Modules:
  0.0 115.7 jit_solution(6856023930659549655)
XLA Ops:
  0.0 0.6 maximum_bitcast_fusion.inverse
  0.6 4.6 %shard_map.55 = (bf16[2,256,2048]{2,1,0:T(8,128)(2,1)}, bf16[2,512,128]{2,1,0:T(8,128)(2,1)}, bf16[2,128,512]{2,1,0:T(8,128)(2,1)}, s32[8,128]{1,0:T(8,128)}) custom-call(s32[8]{0:T(128)} %lengths.1, s32[1]{0:T(128)} %bitcast.first_ref, f32[1,128]{1,0:T(1,128)} %maximum_bitcast_fusion.inverse, bf16[512,1024]{1,0:T(8,128)(2,1)} %queries.1, ...), custom_call_target="tpu_custom_call" | custom-call | tf_op jit(solution)/shard_map/pallas_call | solution.py:81
  5.2 107.3 %shard_map.56 = bf16[512,2048]{1,0:T(8,128)(2,1)} custom-call(s32[8,128]{1,0:T(8,128)} %get-tuple-element.9.bounds, bf16[2,256,2048]{2,1,0:T(8,128)(2,1)} %get-tuple-element.10.qp, bf16[2,512,128]{2,1,0:T(8,128)(2,1)} %get-tuple-element.11.kp, bf16[2,128,512]{2,1,0:T(8,128)(2,1)} %get-tuple-element.12.vp, bf16[1024,8192]{1,0:T(8,128)(2,1)} %w_hbm.1), custom_call_target="tpu_custom_call" | custom-call | tf_op jit(solution)/shard_map/pallas_call | solution.py:501
  112.5 3.2 %copy.7 = bf16[512,2048]{1,0:T(8,128)(2,1)} copy(bf16[512,2048]{1,0:T(8,128)(2,1)} %shard_map.56) | data formatting | bytes 4194304
  (1 shorter events, 0.0 us)
